TPU v7x, 128 devices: a whole 4x4x4 slice. The times are simulated.
128 devices in a mesh: row: 8 (over z, core), col: 16 (over y, x).
Axes of the slice: x: 4, y: 4, z: 4, core: 2. Of those that a mesh axis runs over, the one named last changes fastest.
Arguments:
- hidden_state: bfloat16 [512, 8192], P('col', 'row'), may hold values from -6 to 6
- norm_gain: float32 [8192], P('row'), may hold values from 0.5 to 1.5
- head_weight: bfloat16 [8192, 65536], P('row', 'col'), may hold values from -40 to 40
- targets: int32 [512], replicated, may hold values from 0 to 65535
- gate_act: bfloat16 [512, 26624], P(None, 'col'), may hold values from -6 to 6
- up_act: bfloat16 [512, 26624], P(None, 'col'), may hold values from -6 to 6
Outputs:
- head_grad: bfloat16 [8192, 65536], P('row', 'col')
- grad_hidden: bfloat16 [512, 8192], P('col', 'row')
- down_grad: bfloat16 [26624, 8192], P('col', 'row')
All inputs are finite; a program needn't handle non-finite values.
Results may differ from a plain program's by a relative error of at most 0.024.
Values may be sent and summed in bfloat16 or wider, within the bound.
A program may use at most 128 MiB of HBM per device.

v0:
```python
import jax
import jax.numpy as jnp
from jax import lax
from jax.sharding import PartitionSpec as P

D = 8192


def joined(value, axis, join):
    pieces = jax.tree.map(lambda part: lax.all_gather(part, axis), value)
    head = jax.tree.map(lambda part: part[0], pieces)
    tail = jax.tree.map(lambda part: part[1:], pieces)
    so_far, _ = lax.scan(lambda so_far, piece: (join(so_far, piece), None), head, tail)
    return so_far


def combine(left_part, right_part):
    biggest = jnp.maximum(left_part[0], right_part[0])
    left_scale = jnp.exp(left_part[0] - biggest)
    right_scale = jnp.exp(right_part[0] - biggest)
    return (
        biggest,
        left_part[1] * left_scale + right_part[1] * right_scale,
        left_part[2] * left_scale + right_part[2] * right_scale,
        left_part[3] + right_part[3],
    )


def on_device(hidden_state, norm_gain, head_weight, targets, gate_act, up_act):
    tok_col = hidden_state.shape[0]
    feat_rows = head_weight.shape[0]
    vocab_part = head_weight.shape[1]
    widened = hidden_state.astype(jnp.float32)
    scaled = (norm_gain[None, :] * widened).astype(jnp.bfloat16)
    part_squares = jnp.sum(widened * widened, axis=1)
    tokens_all = tok_col * lax.axis_size("col")
    starting = (
        jnp.zeros((tokens_all, vocab_part), jnp.float32),
        jnp.zeros((tokens_all,), jnp.float32),
        jnp.zeros((tokens_all, feat_rows), jnp.bfloat16),
    )
    pieces = (
        lax.all_gather(scaled, "col", axis=0, tiled=True),
        lax.all_gather(part_squares.astype(jnp.bfloat16), "col", axis=0, tiled=True).astype(
            jnp.float32
        ),
    )
    product = jnp.dot(pieces[0], head_weight, preferred_element_type=jnp.float32)
    partial_squares = lax.dynamic_update_slice_in_dim(starting[1], pieces[1], jnp.int32(0), 0)
    gathered_rows = pieces[0]
    vocab_start = lax.axis_index("col") * vocab_part
    logit_sum, square_sum = (
        lax.psum_scatter(product, "row", scatter_dimension=0, tiled=True),
        lax.psum_scatter(partial_squares, "row", scatter_dimension=0, tiled=True),
    )
    row_targets = lax.dynamic_slice_in_dim(
        targets, lax.axis_index("row") * logit_sum.shape[0], logit_sum.shape[0]
    )
    inv_rms = 1.0 / jnp.sqrt(square_sum / D + 1e-05)
    logits = inv_rms[:, None] * logit_sum
    local_max = jnp.max(logits, axis=1)
    shifted = jnp.exp(logits - local_max[:, None])
    local_sum = jnp.sum(shifted, axis=1)
    local_moment = jnp.sum(shifted * logits, axis=1)
    matches = row_targets[:, None] - vocab_start == jnp.arange(vocab_part, dtype=jnp.int32)[None, :]
    local_target = jnp.sum(jnp.where(matches, logits, 0.0), axis=1)
    top_logit, exp_total, moment, target_logit = joined(
        (local_max, local_sum, local_moment, local_target), "col", combine
    )
    softmax_probs = jnp.exp(logits - top_logit[:, None]) / exp_total[:, None]
    scaled_grad = (inv_rms[:, None] * (softmax_probs - matches.astype(jnp.float32))).astype(
        jnp.bfloat16
    )
    curvature = moment / exp_total - target_logit
    grad_all, inv_all, curv_all = (
        lax.all_gather(scaled_grad, "row", axis=0, tiled=True),
        lax.all_gather(inv_rms.astype(jnp.bfloat16), "row", axis=0, tiled=True).astype(
            inv_rms.dtype
        ),
        lax.all_gather(curvature.astype(jnp.bfloat16), "row", axis=0, tiled=True).astype(
            curvature.dtype
        ),
    )
    head_grad = lax.dot_general(
        gathered_rows, grad_all, (((0,), (0,)), ((), ())), preferred_element_type=jnp.float32
    ).astype(jnp.bfloat16)
    feature_grad = lax.psum_scatter(
        lax.dot_general(
            grad_all, head_weight, (((1,), (1,)), ((), ())), preferred_element_type=jnp.float32
        ).astype(jnp.bfloat16),
        "col",
        scatter_dimension=0,
        tiled=True,
    ).astype(jnp.float32)
    col_start = lax.axis_index("col") * tok_col
    inv_mine = lax.dynamic_slice_in_dim(inv_all, col_start, tok_col)
    curv_mine = lax.dynamic_slice_in_dim(curv_all, col_start, tok_col)
    grad_hidden = (
        norm_gain[None, :] * feature_grad - widened * (inv_mine * inv_mine * curv_mine)[:, None] / D
    ).astype(jnp.bfloat16)
    activation = (jax.nn.silu(gate_act.astype(jnp.float32)) * up_act.astype(jnp.float32)).astype(
        jnp.bfloat16
    )
    down_sum = lax.dot_general(
        activation,
        lax.all_gather(grad_hidden, "col", axis=0, tiled=True),
        (((0,), (0,)), ((), ())),
        preferred_element_type=jnp.float32,
    )
    return (head_grad, grad_hidden, down_sum.astype(jnp.bfloat16))


def solution(mesh):
    in_specs = (P("col", "row"), P("row"), P("row", "col"), P(), P(None, "col"), P(None, "col"))
    out_specs = (P("row", "col"), P("col", "row"), P("col", "row"))
    return jax.shard_map(
        on_device, mesh=mesh, in_specs=in_specs, out_specs=out_specs, check_vma=False
    )
```

profile of v0, /device:TPU:0, one launch (start us, length us, event | category | flops | bytes accessed | tf_op | source)
XLA Modules:
  0.0 368.3 jit_solution(14990205859945968707)
XLA Ops:
  7.2 0.0 all-gather.8.cloned.1.call-start
  7.2 1.6 fusion.19
  8.8 0.0 all-gather.8.cloned.1.call-update
  8.8 0.0 reduce-scatter.3.cloned.1.call-start
  8.9 46.9 %all-gather.8.cloned.1.call-done = bf16[512,1024]{1,0:T(8,128)(2,1)} async-done(((bf16[32,1024]{1,0:T(8,128)(2,1)}), bf16[512,1024]{1,0:T(8,128)(2,1)}) %all-gather.8.cloned.1.call-update) | async-done | bytes 1048592 | tf_op jit(solution)/shard_map/all_gather | solution.py:43
  55.8 11.6 %fusion.30 = f32[512,4096]{1,0:T(8,128)} fusion(bf16[512,1024]{1,0:T(8,128)(2,1)} %all-gather.8.cloned.1.call-done, bf16[1024,4096]{1,0:T(8,128)(2,1)} %param.10), kind=kOutput, calls=%fused_computation.51 | convolution fusion | flops 4294967296 | bytes 17825792 | tf_op jit(solution)/shard_map/dot_general | solution.py:48
  67.4 0.0 copy-start.5
  67.4 0.0 copy-start.2
  67.4 0.0 reduce-scatter.3.cloned.1.call-update
  67.4 0.0 all-gather.10.cloned.1.call-start
  67.5 0.6 copy-done.5
  68.1 0.6 dynamic-slice
  70.0 0.0 copy-done.2
  70.0 0.6 fusion.29
  71.2 0.2 dynamic-update-slice
  71.5 38.1 %all-reduce = bf16[512]{0:T(512)(128)(2,1)S(1)} all-reduce(bf16[512]{0:T(512)(128)(2,1)S(1)} %dynamic-update-slice), channel_id=1, replica_groups=mesh['row'=8,'col'=16] {'col'}, use_global_device_ids=true, to_apply=%add | all-reduce | flops 512 | bytes 2048
  109.6 12.7 %all-reduce.7 = f32[512]{0:T(512)S(1)} all-reduce(bf16[512]{0:T(512)(128)(2,1)S(1)} %all-reduce), channel_id=6, replica_groups=mesh['row'=8,'col'=16] {'row'}, use_global_device_ids=true, to_apply=%region_1.0.clone | all-reduce | flops 512 | bytes 3072
  122.3 0.8 dynamic-slice_subtract_fusion
  123.0 0.1 fusion.27
  123.1 0.0 reduce-scatter.3.cloned.1.call-done
  123.1 1.5 multiply_reduce_fusion.1
  124.6 0.2 dynamic-update-slice.1
  124.8 1.8 multiply_reduce_fusion
  126.7 0.2 dynamic-update-slice.2
  126.9 0.2 dynamic-update-slice.3
  127.1 0.2 dynamic-update-slice.4
  127.3 70.8 %all-reduce.8 = (f32[1024]{0:T(1024)S(1)}, f32[1024]{0:T(1024)S(1)}, f32[1024]{0:T(1024)S(1)}, f32[1024]{0:T(1024)S(1)}) all-reduce(f32[1024]{0:T(1024)S(1)} %dynamic-update-slice.1, f32[1024]{0:T(1024)S(1)} %dynamic-update-slice.2, f32[1024]{0:T(1024)S(1)} %dynamic-update-slice.3, ...), channel_id=2, replica_groups=mesh['row'=8,'col'=16] {'col'}, use_global_device_ids=true, to_apply=%add.1 | all-reduce | flops 4096 | bytes 32768
  198.1 0.1 slice.36
  198.2 0.1 slice.37
  198.3 0.1 slice.38
  198.4 0.1 slice.39
  198.4 0.1 reshape.26
  198.5 0.1 reshape.27
  198.6 0.1 reshape.28
  198.6 0.1 reshape.29
  198.7 1.2 while.16
  199.9 2.4 multiply_convert_fusion
  202.3 0.0 all-gather.10.cloned.1.call-update
  202.3 0.0 copy-start
  202.3 0.0 copy-start.1
  202.4 0.0 reduce-scatter.5.cloned.1.call-start
  202.4 26.4 %all-gather.10.cloned.1.call-done = bf16[512,4096]{1,0:T(8,128)(2,1)} async-done(((bf16[64,4096]{1,0:T(8,128)(2,1)}), bf16[512,4096]{1,0:T(8,128)(2,1)}) %all-gather.10.cloned.1.call-update) | async-done | bytes 4194320 | tf_op jit(solution)/shard_map/all_gather | solution.py:76
  228.8 10.1 %convolution_convert_fusion.2 = bf16[512,1024]{1,0:T(8,128)(2,1)} fusion(bf16[512,4096]{1,0:T(8,128)(2,1)} %all-gather.10.cloned.1.call-done, bf16[1024,4096]{1,0:T(8,128)(2,1)} %param.10), kind=kOutput, calls=%fused_computation.26 | convolution fusion | flops 4295491584 | bytes 13631488 | tf_op jit(solution)/shard_map/dot_general | solution.py:88
  239.0 0.0 reduce-scatter.5.cloned.1.call-update
  239.0 0.0 all-gather.12.cloned.1.call-start
  239.7 0.2 dynamic-update-slice.5
  239.9 0.2 dynamic-update-slice.6
  240.2 13.2 %all-reduce.9 = (bf16[512]{0:T(512)(128)(2,1)S(1)}, bf16[512]{0:T(512)(128)(2,1)S(1)}) all-reduce(bf16[512]{0:T(512)(128)(2,1)S(1)} %dynamic-update-slice.6, bf16[512]{0:T(512)(128)(2,1)S(1)} %dynamic-update-slice.5), channel_id=1, replica_groups=mesh['row'=8,'col'=16] {'row'}, use_global_device_ids=true, to_apply=%add.6 | all-reduce | flops 1024 | bytes 4096
  253.4 0.1 dynamic-slice_multiply_fusion.1
  253.5 58.3 %reduce-scatter.5.cloned.1.call-done = bf16[32,1024]{1,0:T(8,128)(2,1)} async-done(((bf16[512,1024]{1,0:T(8,128)(2,1)}), bf16[32,1024]{1,0:T(8,128)(2,1)}) %reduce-scatter.5.cloned.1.call-update) | async-done | bytes 65552 | tf_op jit(solution)/shard_map/reduce_scatter | solution.py:87
  311.7 0.0 copy-done
  311.7 0.0 copy-done.1
  311.7 1.6 fusion.22
  313.3 0.0 all-gather.12.cloned.1.call-update
  313.3 0.0 copy-start.3
  313.3 0.0 copy-start.4
  313.3 10.6 %convolution_convert_fusion = bf16[1024,4096]{1,0:T(8,128)(2,1)} fusion(bf16[512,1024]{1,0:T(8,128)(2,1)} %all-gather.8.cloned.1.call-done, bf16[512,4096]{1,0:T(8,128)(2,1)} %all-gather.10.cloned.1.call-done), kind=kOutput, calls=%fused_computation.16 | convolution fusion | flops 4299161600 | bytes 13631488 | tf_op jit(solution)/shard_map/dot_general | solution.py:84
  324.0 32.6 %all-gather.12.cloned.1.call-done = bf16[512,1024]{1,0:T(8,128)(2,1)} async-done(((bf16[32,1024]{1,0:T(8,128)(2,1)}), bf16[512,1024]{1,0:T(8,128)(2,1)}) %all-gather.12.cloned.1.call-update) | async-done | bytes 1048592 | tf_op jit(solution)/shard_map/all_gather | solution.py:106
  356.5 0.0 copy-done.3
  356.5 0.0 copy-done.4
  356.5 5.2 %convolution_convert_fusion.1 = bf16[1664,1024]{1,0:T(8,128)(2,1)} fusion(bf16[512,1024]{1,0:T(8,128)(2,1)} %all-gather.12.cloned.1.call-done, bf16[512,1664]{1,0:T(8,128)(2,1)S(1)} %copy-done.3, bf16[512,1664]{1,0:T(8,128)(2,1)S(1)} %copy-done.4), kind=kOutput, calls=%fused_computation.19 | convolution fusion | flops 1753350144 | bytes 7864320 | tf_op jit(solution)/shard_map/dot_general | solution.py:104
  (59 shorter events, 0.9 us)
Async XLA Ops:
  7.2 48.6 %all-gather.8.cloned.1.call-start = ((), (), s32[]{:S(2)}) async-start(), calls=%async_computation.2 | async-start | bytes 1114112 | tf_op jit(solution)/shard_map/all_gather | solution.py:43
  8.8 114.3 %reduce-scatter.3.cloned.1.call-start = ((), (), s32[]{:S(2)}) async-start(), calls=%async_computation.3 | async-start | bytes 9437184 | tf_op jit(solution)/shard_map/reduce_scatter | solution.py:53
  67.4 0.7 copy-start.5
  67.4 2.5 copy-start.2
  67.4 161.4 %all-gather.10.cloned.1.call-start = ((), (), s32[]{:S(2)}) async-start(), calls=%async_computation.4 | async-start | bytes 4718592 | tf_op jit(solution)/shard_map/all_gather | solution.py:76
  202.3 109.4 %copy-start = (bf16[32,1024]{1,0:T(8,128)(2,1)S(1)}, bf16[32,1024]{1,0:T(8,128)(2,1)}, u32[]{:S(2)}) copy-start(bf16[32,1024]{1,0:T(8,128)(2,1)} %param.8) | copy-start | bytes 196612
  202.3 109.4 %copy-start.1 = (f32[1024]{0:T(1024)S(1)}, f32[1024]{0:T(1024)}, u32[]{:S(2)}) copy-start(f32[1024]{0:T(1024)} %param.9) | copy-start | bytes 12292
  202.4 109.4 %reduce-scatter.5.cloned.1.call-start = ((), (), s32[]{:S(2)}) async-start(), calls=%async_computation.5 | async-start | bytes 1114112 | tf_op jit(solution)/shard_map/reduce_scatter | solution.py:87
  239.0 117.5 %all-gather.12.cloned.1.call-start = ((), (), s32[]{:S(2)}) async-start(), calls=%async_computation.6 | async-start | bytes 1114112 | tf_op jit(solution)/shard_map/all_gather | solution.py:106
  313.3 43.2 %copy-start.3 = (bf16[512,1664]{1,0:T(8,128)(2,1)S(1)}, bf16[512,1664]{1,0:T(8,128)(2,1)}, u32[]{:S(2)}) copy-start(bf16[512,1664]{1,0:T(8,128)(2,1)} %param.13) | copy-start | bytes 5111812
  313.3 43.2 %copy-start.4 = (bf16[512,1664]{1,0:T(8,128)(2,1)S(1)}, bf16[512,1664]{1,0:T(8,128)(2,1)}, u32[]{:S(2)}) copy-start(bf16[512,1664]{1,0:T(8,128)(2,1)} %param.12) | copy-start | bytes 5111812
Sparse Core Ops, SparseCore 0:
  10.7 45.0 all-gather.7
  67.6 51.9 reduce-scatter.2
  202.4 26.3 all-gather.9
  239.1 72.5 reduce-scatter.4
  314.5 41.9 all-gather.11
where the time goes:
time: 369 us; the launch traced here: 368 us
  waiting for transfers between devices  164 us (44%)
  blocking collectives  135 us (37%)
  matrix products  37.6 us (10%)
  between operations  16.5 us (4%)
  other arithmetic  10.6 us (3%)
  local copies, waits for them, and re-layouts  4.06 us (1%)
    unnamed x4, blocking collectives  135 us
    reduce_scatter x1, waiting for transfers between devices, on_device(): lax.psum_scatter(lax.dot_general(grad_all, head_weight, (((1,), (1,)), ((...  58.3 us
    all_gather x1, waiting for transfers between devices, on_device(): lax.all_gather(scaled, 'col', axis=0, tiled=True)  46.9 us
    all_gather x1, waiting for transfers between devices, on_device(): lax.all_gather(grad_hidden, 'col', axis=0, tiled=True)  32.6 us
    all_gather x1, waiting for transfers between devices, on_device(): lax.all_gather(scaled_grad, 'row', axis=0, tiled=True)  26.4 us
    dot_general x1, matrix products, on_device(): jnp.dot(pieces[0], head_weight, preferred_element_type=jnp.float32)  11.6 us
    dot_general x1, matrix products, on_device(): lax.dot_general(gathered_rows, grad_all, (((0,), (0,)), ((), ())), prefer...  10.6 us
    dot_general x1, matrix products, on_device(): lax.dot_general(grad_all, head_weight, (((1,), (1,)), ((), ())), preferre...  10.1 us
  transfers between devices with their start and end apart: 5, of which 4 were waited for; matrix products, arithmetic and copies ran while one was open for 4% of the time, Pallas kernels for 0%

commit v1 on v0

v1 whole, which is shorter than its diff:
```python
import jax
import jax.numpy as jnp
from jax import lax
from jax.experimental import pallas as pl
from jax.experimental.pallas import tpu as pltpu
from jax.sharding import PartitionSpec as P

D = 8192
EPS = 1e-05
BF, F32, I16, I32 = jnp.bfloat16, jnp.float32, jnp.int16, jnp.int32
MESH = pl.DeviceIdType.MESH
COLS, ROWS = 16, 8
G = 2
SUB = 16
HALF = SUB * COLS
TAIL = 128
CODES = 32000.0
FINE = 64.0
NT = (((1,), (1,)), ((), ()))


def coded(values):
    most = jnp.maximum(jnp.max(jnp.abs(values), axis=1, keepdims=True), 1e-30)
    level = jnp.ceil(jnp.log2(most) * FINE)
    codes = jnp.round(values * (jnp.exp2(level * (-1.0 / FINE)) * CODES))
    return codes.astype(I32).astype(I16), jnp.broadcast_to(level, (values.shape[0], TAIL)).astype(I32).astype(I16)


def decoded(codes, tail):
    level = tail.astype(I32).astype(F32)[:, 0:1]
    return codes.astype(I32).astype(F32) * (jnp.exp2(level * (1.0 / FINE)) * (1.0 / CODES))


def owner_row(q):
    k, ab, b1, b0 = q // 8, (q // 4) % 2, (q // 2) % 2, q % 2
    s_a = jnp.where(ab == 0, b1, b0)
    s_b = jnp.where(ab == 0, b0, b1)
    return (s_b * 2 + (s_a + s_b) % 2) * 2 + k, ab


def kernel(
    hid, gain, tgt, w_hbm,
    own_out, grad_out, scaled_out, all_out,
    w, ag, sq, inv, part, core, m1s, m1r, m2s, m2r, logit, e, grad, st, fac, fg, rsb, gh,
    w_sem, out_sem, ag_s, ag_r, sq_s, sq_r, inv_s, inv_r, c_s, c_r, z1_s, z1_r, z2_s, z2_r,
    e1_s, e1_r, e2_s, e2_r, e3_s, e3_r, st_s, st_r, fa_s, fa_r, rs_s, rs_r, gh_s, gh_r,
):
    row, col = lax.axis_index("row"), lax.axis_index("col")
    z, k = row // 2, row % 2
    hi = z // 2
    s_a = (hi + z) % 2
    s_b = hi
    width = w.shape[1]
    feats = w.shape[0]
    gw = width // G
    dev_core = (z * 2 + (1 - k), col)
    dev_a = ((z + 1 - 2 * (z % 2)) * 2 + k, col)
    dev_b = (((z + 3 + 2 * (z % 2)) % 4) * 2 + k, col)
    first_side = (s_a, s_b)
    second_side = (s_b, s_a)
    first_dev = (dev_a, dev_b)
    second_dev = (dev_b, dev_a)
    keep1 = [k * 128 + ab * 64 + first_side[ab] * 32 for ab in range(2)]
    send1 = [k * 128 + ab * 64 + (1 - first_side[ab]) * 32 for ab in range(2)]
    own = [keep1[ab] + second_side[ab] * 16 for ab in range(2)]
    send2 = [keep1[ab] + (1 - second_side[ab]) * 16 for ab in range(2)]

    def al(v, n=16):
        return pl.multiple_of(v, n)

    def copy(src, dst, ss, rs, dev):
        return pltpu.make_async_remote_copy(
            src_ref=src, dst_ref=dst, send_sem=ss, recv_sem=rs, device_id=dev, device_id_type=MESH
        )

    def col_dev(i):
        return (row, lax.rem(col + i, COLS))

    def row_dev(i):
        return (lax.rem(row + i, ROWS), col)

    def each(n, fn):
        def body(i, carry):
            fn(i)
            return carry

        lax.fori_loop(1, n, body, 0)

    def c_ag(h, i):
        ref = ag.at[h, pl.ds(al(col * SUB), SUB)]
        return copy(ref, ref, ag_s.at[h, i], ag_r.at[h, i], col_dev(i))

    def c_sq(i):
        return copy(sq.at[row], sq.at[row], sq_s.at[i], sq_r.at[i], row_dev(i))

    def c_inv(i):
        return copy(inv.at[col], inv.at[col], inv_s.at[i], inv_r.at[i], col_dev(i))

    def c_core(h, g):
        return copy(part.at[h, g, pl.ds(al((1 - k) * 128), 128)], core.at[h, g], c_s.at[h, g], c_r.at[h, g], dev_core)

    def c_z1(h, g, ab):
        return copy(m1s.at[h, g, ab], m1r.at[h, g, ab], z1_s.at[h, g, ab], z1_r.at[h, g, ab], first_dev[ab])

    def c_z2(h, g, ab):
        return copy(m2s.at[h, g, ab], m2r.at[h, g, ab], z2_s.at[h, g, ab], z2_r.at[h, g, ab], second_dev[ab])

    def c_e1(h, ab):
        ref = e.at[h, pl.ds(al(own[ab]), 16)]
        return copy(ref, ref, e1_s.at[h, ab], e1_r.at[h, ab], second_dev[ab])

    def c_e2(h, ab):
        ref = e.at[h, pl.ds(al(keep1[ab]), 32)]
        return copy(ref, ref, e2_s.at[h, ab], e2_r.at[h, ab], first_dev[ab])

    def c_e3(h):
        ref = e.at[h, pl.ds(al(k * 128), 128)]
        return copy(ref, ref, e3_s.at[h], e3_r.at[h], dev_core)

    def c_st(h, i):
        return copy(st.at[h, col], st.at[h, col], st_s.at[h, i], st_r.at[h, i], col_dev(i))

    def c_fa(h, i):
        return copy(fac.at[h, row], fac.at[h, row], fa_s.at[h, i], fa_r.at[h, i], row_dev(i))

    def c_rs(h, i):
        peer = lax.rem(col + i, COLS)
        return copy(fg.at[h, pl.ds(al(peer * SUB), SUB)], rsb.at[h, col], rs_s.at[h, i], rs_r.at[h, i], col_dev(i))

    def c_gh(h, i):
        ref = gh.at[pl.ds(al(col * 32 + h * SUB), SUB)]
        return copy(ref, ref, gh_s.at[h, i], gh_r.at[h, i], col_dev(i))

    def logits_part(h, g):
        @pl.loop(0, gw // 512)
        def _(n):
            cols = pl.ds(al(n * 512, 512), 512)
            wide = pl.ds(al(g * gw + n * 512, 512), 512)
            part[h, g, :, cols] = jnp.dot(ag[h], w[:, wide], preferred_element_type=F32)

        c_core(h, g).start()

    def reduce_core(h, g):
        c_core(h, g).wait_recv()
        for ab in range(2):
            for s in range(2):
                at = send1[ab] + s * 16
                v = part[h, g, pl.ds(al(at), 16)] + core[h, g, pl.ds(al(at - k * 128), 16)]
                m1s[h, g, ab, s * 16:s * 16 + 16, 0:gw], m1s[h, g, ab, s * 16:s * 16 + 16, gw:] = coded(v)
            c_z1(h, g, ab).start()
        for ab in range(2):
            for s in range(2):
                at = keep1[ab] + s * 16
                part[h, g, pl.ds(al(at), 16)] += core[h, g, pl.ds(al(at - k * 128), 16)]

    def reduce_first(h, g):
        for ab in range(2):
            c_z1(h, g, ab).wait_recv()
            there = pl.ds(al((1 - second_side[ab]) * 16), 16)
            v = part[h, g, pl.ds(al(send2[ab]), 16)] + decoded(m1r[h, g, ab, there, 0:gw], m1r[h, g, ab, there, gw:])
            m2s[h, g, ab, :, 0:gw], m2s[h, g, ab, :, gw:] = coded(v)
            c_z2(h, g, ab).start()
        for ab in range(2):
            here = pl.ds(al(second_side[ab] * 16), 16)
            part[h, g, pl.ds(al(own[ab]), 16)] += decoded(m1r[h, g, ab, here, 0:gw], m1r[h, g, ab, here, gw:])

    def reduce_second(h, g):
        for ab in range(2):
            c_z2(h, g, ab).wait_recv()
            logit[h, ab * 16:ab * 16 + 16, g * gw:(g + 1) * gw] = part[h, g, pl.ds(al(own[ab]), 16)] + decoded(
                m2r[h, g, ab, :, 0:gw], m2r[h, g, ab, :, gw:]
            )

    vocab_start = col * width
    lane = lax.broadcasted_iota(I32, (16, 128), 1)
    cb = min(1024, width)

    def softmax_part(h):
        for ab in range(2):
            rows = slice(ab * 16, ab * 16 + 16)
            q = own[ab] // 16
            inv_col = inv[q, h * 16:h * 16 + 16, 0:1]
            t_col = tgt[h, pl.ds(al(own[ab]), 16), 0:1] - vocab_start
            top = jnp.full((16, 1), -jnp.inf, F32)
            for n in range(width // cb):
                cols = slice(n * cb, (n + 1) * cb)
                x = logit[h, rows, cols] * inv_col
                top = jnp.maximum(top, jnp.max(x, axis=1, keepdims=True))
            total = jnp.zeros((16, 1), F32)
            moment = jnp.zeros((16, 1), F32)
            target = jnp.zeros((16, 1), F32)
            for n in range(width // cb):
                cols = slice(n * cb, (n + 1) * cb)
                x = logit[h, rows, cols] * inv_col
                y = jnp.exp(x - top)
                e[h, pl.ds(al(own[ab]), 16), cols] = y.astype(BF)
                total += jnp.sum(y, axis=1, keepdims=True)
                moment += jnp.sum(y * x, axis=1, keepdims=True)
                ids = lax.broadcasted_iota(I32, (16, cb), 1) + n * cb
                target += jnp.sum(jnp.where(ids == t_col, x, 0.0), axis=1, keepdims=True)
            c_e1(h, ab).start()
            st[h, col, rows, :] = jnp.where(
                lane == 0, top, jnp.where(lane == 1, total, jnp.where(lane == 2, moment, target))
            )
        each(COLS, lambda i: c_st(h, i).start())

    def spread_first(h):
        for ab in range(2):
            c_e1(h, ab).wait_recv()
            c_e2(h, ab).start()

    def spread_second(h):
        for ab in range(2):
            c_e2(h, ab).wait_recv()
        c_e3(h).start()

    def combine(h):
        each(COLS, lambda i: c_st(h, i).wait_recv())
        top = st[h, 0, :, 0:1]
        for j in range(1, COLS):
            top = jnp.maximum(top, st[h, j, :, 0:1])
        total, moment, target = (jnp.zeros((32, 1), F32) for _ in range(3))
        for j in range(COLS):
            s = st[h, j]
            scale = jnp.exp(s[:, 0:1] - top)
            total += s[:, 1:2] * scale
            moment += s[:, 2:3] * scale
            target += s[:, 3:4]
        mine = jnp.exp(st[h, col, :, 0:1] - top) / total
        curv = moment / total - target
        for ab in range(2):
            rows = slice(ab * 16, ab * 16 + 16)
            inv_col = inv[own[ab] // 16, h * 16:h * 16 + 16, 0:1]
            fac[h, row, rows, :] = jnp.where(lane == 0, mine[rows] * inv_col, curv[rows])
        each(ROWS, lambda i: c_fa(h, i).start())

    def gradient(h):
        c_e3(h).wait_recv()
        each(ROWS, lambda i: c_fa(h, i).wait_recv())

        def group(q, carry):
            r, ab = owner_row(q)
            f_col = fac[h, r, pl.ds(al(ab * 16), 16), 0:1]
            inv_col = inv[q, h * 16:h * 16 + 16, 0:1]
            rows = pl.ds(al(q * 16), 16)
            t_col = tgt[h, rows, 0:1] - vocab_start
            for n in range(width // cb):
                cols = slice(n * cb, (n + 1) * cb)
                ids = lax.broadcasted_iota(I32, (16, cb), 1) + n * cb
                y = e[h, rows, cols].astype(F32) * f_col - jnp.where(ids == t_col, inv_col, 0.0)
                grad[h, rows, cols] = y.astype(BF)
            return carry

        lax.fori_loop(0, COLS, group, 0)
        pltpu.make_async_copy(grad.at[h], grad_out.at[h], out_sem.at[h]).start()

        @pl.loop(0, feats // 256)
        def _(n):
            rows = pl.ds(al(n * 256, 256), 256)
            y = lax.dot_general(grad[h], w[rows, :], NT, preferred_element_type=F32)
            fg[h, :, rows] = y.astype(BF)

        each(COLS, lambda i: c_rs(h, i).start())

    def residual(h):
        each(COLS, lambda i: c_rs(h, i).wait_recv())
        total = fg[h, pl.ds(al(col * SUB), SUB), :].astype(F32)

        def add(i, total):
            return total + rsb[h, lax.rem(col + i, COLS)].astype(F32)

        total = lax.fori_loop(1, COLS, add, total)
        r, ab = owner_row(col)
        curv = fac[h, r, pl.ds(al(ab * 16), 16), 1:2]
        inv_col = inv[col, h * 16:h * 16 + 16, 0:1]
        x = hid[h * 16:h * 16 + 16, :].astype(F32)
        y = (gain[...] * total - x * (inv_col * inv_col * curv) / D).astype(BF)
        gh[pl.ds(al(col * 32 + h * SUB), SUB), :] = y
        own_out[h * 16:h * 16 + 16, :] = y
        each(COLS, lambda i: c_gh(h, i).start())

    load = pltpu.make_async_copy(w_hbm, w, w_sem)
    load.start()
    barrier = pltpu.get_barrier_semaphore()
    each(COLS, lambda i: pl.semaphore_signal(barrier, inc=1, device_id=col_dev(i), device_id_type=MESH))
    each(ROWS, lambda i: pl.semaphore_signal(barrier, inc=1, device_id=row_dev(i), device_id_type=MESH))
    for h in range(2):
        x = hid[h * 16:h * 16 + 16, :].astype(F32)
        ag[h, pl.ds(al(col * SUB), SUB), :] = (gain[...] * x).astype(BF)
        sq[row, h * 16:h * 16 + 16, :] = jnp.broadcast_to(jnp.sum(x * x, axis=1, keepdims=True), (16, 128))
    pl.semaphore_wait(barrier, COLS + ROWS - 2)
    each(COLS, lambda i: c_ag(0, i).start())
    each(ROWS, lambda i: c_sq(i).start())
    each(COLS, lambda i: c_ag(1, i).start())
    each(ROWS, lambda i: c_sq(i).wait_recv())
    squares = sq[0]
    for r in range(1, ROWS):
        squares = squares + sq[r]
    inv[col] = 1.0 / jnp.sqrt(squares / D + EPS)
    each(COLS, lambda i: c_inv(i).start())
    load.wait()
    each(COLS, lambda i: c_ag(0, i).wait_recv())
    for g in range(G):
        logits_part(0, g)
    each(COLS, lambda i: c_ag(1, i).wait_recv())
    pltpu.make_async_copy(ag, scaled_out, out_sem.at[2]).start()
    for g in range(G):
        reduce_core(0, g)
        logits_part(1, g)
    for g in range(G):
        reduce_first(0, g)
        reduce_core(1, g)
    each(COLS, lambda i: c_inv(i).wait_recv())
    for g in range(G):
        reduce_second(0, g)
    softmax_part(0)
    for g in range(G):
        reduce_first(1, g)
    spread_first(0)
    for g in range(G):
        reduce_second(1, g)
    softmax_part(1)
    combine(0)
    spread_second(0)
    spread_first(1)
    combine(1)
    gradient(0)
    spread_second(1)
    residual(0)
    gradient(1)
    residual(1)
    for h in range(2):
        each(COLS, lambda i: c_gh(h, i).wait_recv())
    last = pltpu.make_async_copy(gh, all_out, out_sem.at[3])
    last.start()
    each(ROWS, lambda i: c_sq(i).wait_send())
    each(COLS, lambda i: c_inv(i).wait_send())
    for h in range(2):
        each(COLS, lambda i: c_ag(h, i).wait_send())
        each(COLS, lambda i: c_st(h, i).wait_send())
        each(ROWS, lambda i: c_fa(h, i).wait_send())
        each(COLS, lambda i: c_rs(h, i).wait_send())
        each(COLS, lambda i: c_gh(h, i).wait_send())
        for g in range(G):
            c_core(h, g).wait_send()
            for ab in range(2):
                c_z1(h, g, ab).wait_send()
                c_z2(h, g, ab).wait_send()
        for ab in range(2):
            c_e1(h, ab).wait_send()
            c_e2(h, ab).wait_send()
        c_e3(h).wait_send()
        pltpu.make_async_copy(grad.at[h], grad_out.at[h], out_sem.at[h]).wait()
    pltpu.make_async_copy(ag, scaled_out, out_sem.at[2]).wait()
    last.wait()


def on_device(hidden_state, norm_gain, head_weight, targets, gate_act, up_act):
    feats, width = head_weight.shape
    gw = width // G
    tokens = 2 * HALF
    order = targets.reshape(COLS, 2, SUB).transpose(1, 0, 2).reshape(2, HALF, 1)
    order = jnp.broadcast_to(order, (2, HALF, 128))
    vm, hbm = pl.BlockSpec(memory_space=pltpu.VMEM), pl.BlockSpec(memory_space=pl.ANY)
    dma = pltpu.SemaphoreType.DMA

    def pair(*shape):
        return [dma(shape), dma(shape)]

    grad_hidden, grad, scaled, resid = pl.pallas_call(
        kernel,
        out_shape=(
            jax.ShapeDtypeStruct(hidden_state.shape, BF),
            jax.ShapeDtypeStruct((2, HALF, width), BF),
            jax.ShapeDtypeStruct((2, HALF, feats), BF),
            jax.ShapeDtypeStruct((tokens, feats), BF),
        ),
        in_specs=[vm, vm, vm, hbm],
        out_specs=(vm, hbm, hbm, hbm),
        scratch_shapes=[
            pltpu.VMEM((feats, width), BF),
            pltpu.VMEM((2, HALF, feats), BF),
            pltpu.VMEM((ROWS, 32, 128), F32),
            pltpu.VMEM((COLS, 32, 128), F32),
            pltpu.VMEM((2, G, HALF, gw), F32),
            pltpu.VMEM((2, G, HALF // 2, gw), F32),
            pltpu.VMEM((2, G, 2, 32, gw + TAIL), I16),
            pltpu.VMEM((2, G, 2, 32, gw + TAIL), I16),
            pltpu.VMEM((2, G, 2, 16, gw + TAIL), I16),
            pltpu.VMEM((2, G, 2, 16, gw + TAIL), I16),
            pltpu.VMEM((2, 32, width), F32),
            pltpu.VMEM((2, HALF, width), BF),
            pltpu.VMEM((2, HALF, width), BF),
            pltpu.VMEM((2, COLS, 32, 128), F32),
            pltpu.VMEM((2, ROWS, 32, 128), F32),
            pltpu.VMEM((2, HALF, feats), BF),
            pltpu.VMEM((2, COLS, SUB, feats), BF),
            pltpu.VMEM((tokens, feats), BF),
            dma, dma((4,)),
            *pair(2, COLS), *pair(ROWS), *pair(COLS), *pair(2, G), *pair(2, G, 2), *pair(2, G, 2),
            *pair(2, 2), *pair(2, 2), *pair(2), *pair(2, COLS), *pair(2, ROWS), *pair(2, COLS), *pair(2, COLS),
        ],
        compiler_params=pltpu.CompilerParams(
            collective_id=0, has_side_effects=True, vmem_limit_bytes=58 * 2**20
        ),
        name="head_backward",
    )(hidden_state, norm_gain.reshape(1, feats), order, head_weight)
    head_grad = lax.dot_general(
        scaled.reshape(tokens, feats), grad.reshape(tokens, width), (((0,), (0,)), ((), ())),
        preferred_element_type=F32,
    ).astype(BF)
    activation = (jax.nn.silu(gate_act.astype(F32)) * up_act.astype(F32)).astype(BF)
    down_grad = lax.dot_general(
        activation, resid, (((0,), (0,)), ((), ())), preferred_element_type=F32
    ).astype(BF)
    return head_grad, grad_hidden, down_grad


def solution(mesh):
    in_specs = (P("col", "row"), P("row"), P("row", "col"), P(), P(None, "col"), P(None, "col"))
    out_specs = (P("row", "col"), P("col", "row"), P("col", "row"))
    return jax.shard_map(
        on_device, mesh=mesh, in_specs=in_specs, out_specs=out_specs, check_vma=False
    )
```

time: 369 us -> 118 us (0.32)
  waiting for transfers between devices: 164 us -> 0 us
  blocking collectives: 135 us -> 0 us
  Pallas kernels: 0 us -> 100 us
  matrix products: 37.6 us -> 14.6 us
  between operations: 16.5 us -> 0.69 us
  other arithmetic: 10.6 us -> 0 us
    unnamed x4 -> x0, blocking collectives: 135 us -> none
    all_gather x3 -> x0, waiting for transfers between devices: 106 us -> none  [the longest x1 46.9 us: on_device(): lax.all_gather(scaled, 'col', axis=0, tiled=True)]
    pallas_call x0 -> x1, Pallas kernels: none -> 100 us  [on_device(): pl.pallas_call(kernel, out_shape=(jax.ShapeDtypeStruct(hidden_state.shape...]
    reduce_scatter x2 -> x0, waiting for transfers between devices: 58.3 us -> none  [the longest x1 58.3 us: on_device(): lax.psum_scatter(lax.dot_general(grad_all, head_weight, (((1,), (1,)), ((...]
    dot_general x4 -> x2, matrix products: 37.6 us -> 14.6 us  [the longest x1 10.6 us: on_device(): lax.dot_general(scaled.reshape(tokens, feats), grad.reshape(tokens, width...]
    convert_element_type x6 -> x0, other arithmetic: 4.07 us -> none  [the longest x1 2.43 us: on_device(): (inv_rms[:, None] * (softmax_probs - matches.astype(jnp.float32))).astype...]
  transfers between devices with their start and end apart: 5 -> 0, of which waited for: 4 -> 0; matrix products, arithmetic and copies ran while one was open for 4% -> 0% of each run, Pallas kernels for 0% -> 0%
where the time goes in v1:
time: 118 us
  Pallas kernels  100 us (85%)
  matrix products  14.6 us (12%)
  local copies, waits for them, and re-layouts  2.35 us (2%)
    pallas_call x1, Pallas kernels, on_device(): pl.pallas_call(kernel, out_shape=(jax.ShapeDtypeStruct(hidden_state.shape...  100 us
    dot_general x1, matrix products, on_device(): lax.dot_general(scaled.reshape(tokens, feats), grad.reshape(tokens, width...  10.6 us
    dot_general x1, matrix products, on_device(): lax.dot_general(activation, resid, (((0,), (0,)), ((), ())), preferred_el...  4.01 us

profile of v1, /device:TPU:0, one launch (start us, length us, event | category | flops | bytes accessed | tf_op | source)
XLA Modules:
  0.0 118.1 jit_solution(8300988123813488389)
XLA Ops:
  0.6 0.8 reshape.17
  1.4 0.1 broadcast_in_dim.7
  1.5 0.8 broadcast_in_dim.8.tgt
  2.3 100.4 %head_backward.1 = (bf16[32,1024]{1,0:T(8,128)(2,1)}, bf16[2,256,4096]{2,1,0:T(8,128)(2,1)}, bf16[2,256,1024]{2,1,0:T(8,128)(2,1)}, bf16[512,1024]{1,0:T(8,128)(2,1)}) custom-call(bf16[32,1024]{1,0:T(8,128)(2,1)} %hid.1, f32[1,1024]{1,0:T(1,128)} %bitcast.8, s32[2,256,128]{2,1,0:T(8,128)} %broadcast_in_dim.8.tgt, bf16[1024,4096]{1,0:T(8,128)(2,1)} %w_hbm.1), custom_call_target="tpu_custom_call" | custom-call | tf_op jit(solution)/shard_map/head_backward/pallas_call | solution.py:370
  102.7 0.0 copy-start.1
  102.8 0.0 copy-start.2
  102.8 0.0 copy-start.3
  102.8 10.6 %bitcast_convert_fusion = bf16[1024,4096]{1,0:T(8,128)(2,1)} fusion(bf16[2,256,1024]{2,1,0:T(8,128)(2,1)} %get-tuple-element.7, bf16[2,256,4096]{2,1,0:T(8,128)(2,1)} %get-tuple-element.8), kind=kOutput, calls=%fused_computation | convolution fusion | flops 4299161600 | bytes 13631488 | tf_op jit(solution)/shard_map/dot_general | solution.py:408
  113.4 0.0 copy-done.1
  113.4 0.0 copy-done.2
  113.4 0.0 copy-done.3
  113.4 0.0 copy-start
  113.4 4.0 %convolution_convert_fusion = bf16[1664,1024]{1,0:T(8,128)(2,1)} fusion(bf16[512,1024]{1,0:T(8,128)(2,1)S(1)} %copy-done.3, bf16[512,1664]{1,0:T(8,128)(2,1)S(1)} %copy-done.1, bf16[512,1664]{1,0:T(8,128)(2,1)S(1)} %copy-done.2), kind=kOutput, calls=%fused_computation.3 | convolution fusion | flops 1753350144 | bytes 7864320 | tf_op jit(solution)/shard_map/dot_general | solution.py:413
  117.4 0.0 copy-done
  117.4 0.6 copy.15
  (1 shorter events, 0.0 us)
Async XLA Ops:
  102.7 10.7 %copy-start.1 = (bf16[512,1664]{1,0:T(8,128)(2,1)S(1)}, bf16[512,1664]{1,0:T(8,128)(2,1)}, u32[]{:S(2)}) copy-start(bf16[512,1664]{1,0:T(8,128)(2,1)} %param.11) | copy-start | bytes 5111812
  102.8 10.6 %copy-start.2 = (bf16[512,1664]{1,0:T(8,128)(2,1)S(1)}, bf16[512,1664]{1,0:T(8,128)(2,1)}, u32[]{:S(2)}) copy-start(bf16[512,1664]{1,0:T(8,128)(2,1)} %param.10) | copy-start | bytes 5111812
  102.8 10.6 %copy-start.3 = (bf16[512,1024]{1,0:T(8,128)(2,1)S(1)}, bf16[512,1024]{1,0:T(8,128)(2,1)}, u32[]{:S(2)}) copy-start(bf16[512,1024]{1,0:T(8,128)(2,1)} %get-tuple-element.10) | copy-start | bytes 3145732
  113.4 4.0 %copy-start = (bf16[32,1024]{1,0:T(8,128)(2,1)S(1)}, bf16[32,1024]{1,0:T(8,128)(2,1)}, u32[]{:S(2)}) copy-start(bf16[32,1024]{1,0:T(8,128)(2,1)} %get-tuple-element.15) | copy-start | bytes 196612

commit v2 on v1

v2 whole, which is shorter than its diff:
```python
import jax
import jax.numpy as jnp
from jax import lax
from jax.experimental import pallas as pl
from jax.experimental.pallas import tpu as pltpu
from jax.sharding import PartitionSpec as P

D = 8192
EPS = 1e-05
BF, F32, I16, I32 = jnp.bfloat16, jnp.float32, jnp.int16, jnp.int32
MESH = pl.DeviceIdType.MESH
COLS, ROWS = 16, 8
SIDE = 4
PIECE = 512
G = 2
SUB = 16
HALF = SUB * COLS
TAIL = 128
CODES = 32000.0
FINE = 64.0
STOP = None
NT = (((1,), (1,)), ((), ()))


def coded(values):
    most = jnp.maximum(jnp.max(jnp.abs(values), axis=1, keepdims=True), 1e-30)
    level = jnp.ceil(jnp.log2(most) * FINE)
    codes = jnp.round(values * (jnp.exp2(level * (-1.0 / FINE)) * CODES))
    return codes.astype(I32).astype(I16), jnp.broadcast_to(level, (values.shape[0], TAIL)).astype(I32).astype(I16)


def decoded(codes, tail):
    level = tail.astype(I32).astype(F32)[:, 0:1]
    return codes.astype(I32).astype(F32) * (jnp.exp2(level * (1.0 / FINE)) * (1.0 / CODES))


def owner_row(q):
    k, ab, b1, b0 = q // 8, (q // 4) % 2, (q // 2) % 2, q % 2
    s_a = jnp.where(ab == 0, b1, b0)
    s_b = jnp.where(ab == 0, b0, b1)
    return (s_b * 2 + (s_a + s_b) % 2) * 2 + k, ab


def kernel(
    hid_hbm, gain_hbm, tgt_hbm, w_hbm, gate_hbm, up_hbm,
    own_out, grad_a, grad_b, grad_c, grad_d, scaled_out, all_out, act_out,
    hid, gain, tgt_in, w, gate, up, act, turned, tgt, ag, sq, inv, part, core, m1s, m1r, m2s, m2r, logit, e, grad, st, fac, fg, ra, rb, rc, rd, gh,
    in_sem, out_sem, sq_s, sq_r, inv_s, inv_r, c_s, c_r, z1_s, z1_r, z2_s, z2_r,
    e1_s, e1_r, e2_s, e2_r, e3_s, e3_r, st_s, st_r, fa_s, fa_r,
    aa_s, aa_r, ab_s, ab_r, ac_s, ac_r, ad_s, ad_r, ra_s, ra_r, rb_s, rb_r, rc_s, rc_r, rd_s, rd_r,
    ga_s, ga_r, gb_s, gb_r, gc_s, gc_r, gd_s, gd_r,
):
    row, col = lax.axis_index("row"), lax.axis_index("col")
    z, k = row // 2, row % 2
    hi = z // 2
    s_a = (hi + z) % 2
    s_b = hi
    width = w.shape[1]
    feats = w.shape[0]
    gw = width // G
    hf = feats // 2
    dev_core = (z * 2 + (1 - k), col)
    dev_a = ((z + 1 - 2 * (z % 2)) * 2 + k, col)
    dev_b = (((z + 3 + 2 * (z % 2)) % 4) * 2 + k, col)
    first_side = (s_a, s_b)
    second_side = (s_b, s_a)
    first_dev = (dev_a, dev_b)
    second_dev = (dev_b, dev_a)
    keep1 = [k * 128 + ab * 64 + first_side[ab] * 32 for ab in range(2)]
    send1 = [k * 128 + ab * 64 + (1 - first_side[ab]) * 32 for ab in range(2)]
    own = [keep1[ab] + second_side[ab] * 16 for ab in range(2)]
    send2 = [keep1[ab] + (1 - second_side[ab]) * 16 for ab in range(2)]

    def al(v, n=16):
        return pl.multiple_of(v, n)

    started, coming, stores = [], [], []
    loads = [(w_hbm, w, in_sem.at[0]), (gate_hbm, gate, in_sem.at[1]), (up_hbm, up, in_sem.at[2])]
    loads += [(hid_hbm, hid, in_sem.at[3]), (gain_hbm, gain, in_sem.at[4]), (tgt_hbm, tgt_in, in_sem.at[5])]

    def copy(src, dst, ss, rs, dev):
        return pltpu.make_async_remote_copy(
            src_ref=src, dst_ref=dst, send_sem=ss, recv_sem=rs, device_id=dev, device_id_type=MESH
        )

    def send(make, *key, peers=None):
        started.append((make, key, peers))
        coming.append((make, key, peers))
        if peers:
            each(peers, lambda i: make(*key, i).start())
        else:
            make(*key).start()

    def arrive(make, *key, peers=None):
        coming.remove((make, key, peers))
        if peers:
            each(peers, lambda i: make(*key, i).wait_recv())
        else:
            make(*key).wait_recv()

    def store(src, dst, sem):
        stores.append((src, dst, sem))
        pltpu.make_async_copy(src, dst, sem).start()

    def stored(n):
        src, dst, sem = loads[n]
        del stores[[d is dst for _, d, _ in stores].index(True)]
        pltpu.make_async_copy(src, dst, sem).wait()

    def left(make, key, peers):
        if peers:
            each(peers, lambda i: make(*key, i).wait_send())
        else:
            make(*key).wait_send()

    def col_dev(i):
        return (row, lax.rem(col + i, COLS))

    x, y = col % SIDE, col // SIDE

    def x_dev(i):
        return (row, y * SIDE + lax.rem(x + i, SIDE))

    def y_dev(i):
        return (row, lax.rem(y + i, SIDE) * SIDE + x)

    def row_dev(i):
        return (lax.rem(row + i, ROWS), col)

    def each(n, fn):
        def body(i, carry):
            fn(i)
            return carry

        lax.fori_loop(1, n, body, 0)

    def c_aa(h, i):
        ref = ag.at[h, y, x, :, 0:hf]
        return copy(ref, ref, aa_s.at[h, i], aa_r.at[h, i], x_dev(i))

    def c_ab(h, i):
        ref = ag.at[h, y, x, :, hf:feats]
        return copy(ref, ref, ab_s.at[h, i], ab_r.at[h, i], y_dev(i))

    def c_ac(h, i):
        ref = ag.at[h, y, :, :, 0:hf]
        return copy(ref, ref, ac_s.at[h, i], ac_r.at[h, i], y_dev(i))

    def c_ad(h, i):
        ref = ag.at[h, :, x, :, hf:feats]
        return copy(ref, ref, ad_s.at[h, i], ad_r.at[h, i], x_dev(i))

    def c_sq(i):
        return copy(sq.at[row], sq.at[row], sq_s.at[i], sq_r.at[i], row_dev(i))

    def c_inv(i):
        return copy(inv.at[col], inv.at[col], inv_s.at[i], inv_r.at[i], col_dev(i))

    def c_core(h, g, n):
        cols = pl.ds(al(n * PIECE, PIECE), PIECE)
        return copy(
            part.at[h, g, pl.ds(al((1 - k) * 128), 128), cols], core.at[h, g, :, cols],
            c_s.at[h, g, n], c_r.at[h, g, n], dev_core,
        )

    def c_z1(h, g, ab):
        return copy(m1s.at[h, g, ab], m1r.at[h, g, ab], z1_s.at[h, g, ab], z1_r.at[h, g, ab], first_dev[ab])

    def c_z2(h, g, ab):
        return copy(m2s.at[h, g, ab], m2r.at[h, g, ab], z2_s.at[h, g, ab], z2_r.at[h, g, ab], second_dev[ab])

    def c_e1(h, ab):
        ref = e.at[h, pl.ds(al(own[ab]), 16)]
        return copy(ref, ref, e1_s.at[h, ab], e1_r.at[h, ab], second_dev[ab])

    def c_e2(h, ab):
        ref = e.at[h, pl.ds(al(keep1[ab]), 32)]
        return copy(ref, ref, e2_s.at[h, ab], e2_r.at[h, ab], first_dev[ab])

    def c_e3(h, ab, late):
        ref = e.at[h, pl.ds(al((send1 if late else keep1)[ab]), 32)]
        return copy(ref, ref, e3_s.at[h, ab, late], e3_r.at[h, ab, late], dev_core)

    def c_st(h, i):
        return copy(st.at[h, col], st.at[h, col], st_s.at[h, i], st_r.at[h, i], col_dev(i))

    def c_fa(h, i):
        return copy(fac.at[h, row], fac.at[h, row], fa_s.at[h, i], fa_r.at[h, i], row_dev(i))

    def c_ra(h, i):
        return copy(fg.at[h, :, lax.rem(x + i, SIDE), :, 0:hf], ra.at[h, i], ra_s.at[h, i], ra_r.at[h, i], x_dev(i))

    def c_rb(h, i):
        return copy(fg.at[h, lax.rem(y + i, SIDE), :, :, hf:feats], rb.at[h, i], rb_s.at[h, i], rb_r.at[h, i], y_dev(i))

    def c_rc(h, i):
        return copy(ra.at[h, 0, lax.rem(y + i, SIDE)], rc.at[h, i], rc_s.at[h, i], rc_r.at[h, i], y_dev(i))

    def c_rd(h, i):
        return copy(rb.at[h, 0, lax.rem(x + i, SIDE)], rd.at[h, i], rd_s.at[h, i], rd_r.at[h, i], x_dev(i))

    def c_ga(h, i):
        ref = gh.at[y, x, h, :, 0:hf]
        return copy(ref, ref, ga_s.at[h, i], ga_r.at[h, i], x_dev(i))

    def c_gb(h, i):
        ref = gh.at[y, x, h, :, hf:feats]
        return copy(ref, ref, gb_s.at[h, i], gb_r.at[h, i], y_dev(i))

    def c_gc(h, i):
        ref = gh.at[y, :, h, :, 0:hf]
        return copy(ref, ref, gc_s.at[h, i], gc_r.at[h, i], y_dev(i))

    def c_gd(h, i):
        ref = gh.at[:, x, h, :, hf:feats]
        return copy(ref, ref, gd_s.at[h, i], gd_r.at[h, i], x_dev(i))

    def logits_part(h, g):
        for n in range(gw // PIECE):
            cols = slice(n * PIECE, (n + 1) * PIECE)
            wide = slice(g * gw + n * PIECE, g * gw + (n + 1) * PIECE)
            part[h, g, :, cols] = jnp.dot(ag[h].reshape(HALF, feats), w[:, wide], preferred_element_type=F32)
            send(c_core, h, g, n)

    def reduce_core(h, g):
        for n in range(gw // PIECE):
            arrive(c_core, h, g, n)
        for ab in range(2):
            for s in range(2):
                at = send1[ab] + s * 16
                v = part[h, g, pl.ds(al(at), 16)] + core[h, g, pl.ds(al(at - k * 128), 16)]
                m1s[h, g, ab, s * 16:s * 16 + 16, 0:gw], m1s[h, g, ab, s * 16:s * 16 + 16, gw:] = coded(v)
            send(c_z1, h, g, ab)
        for ab in range(2):
            for s in range(2):
                at = keep1[ab] + s * 16
                part[h, g, pl.ds(al(at), 16)] += core[h, g, pl.ds(al(at - k * 128), 16)]

    def reduce_first(h, g):
        for ab in range(2):
            arrive(c_z1, h, g, ab)
            there = pl.ds(al((1 - second_side[ab]) * 16), 16)
            v = part[h, g, pl.ds(al(send2[ab]), 16)] + decoded(m1r[h, g, ab, there, 0:gw], m1r[h, g, ab, there, gw:])
            m2s[h, g, ab, :, 0:gw], m2s[h, g, ab, :, gw:] = coded(v)
            send(c_z2, h, g, ab)
        for ab in range(2):
            here = pl.ds(al(second_side[ab] * 16), 16)
            part[h, g, pl.ds(al(own[ab]), 16)] += decoded(m1r[h, g, ab, here, 0:gw], m1r[h, g, ab, here, gw:])

    def reduce_second(h, g):
        for ab in range(2):
            arrive(c_z2, h, g, ab)
            logit[h, ab * 16:ab * 16 + 16, g * gw:(g + 1) * gw] = part[h, g, pl.ds(al(own[ab]), 16)] + decoded(
                m2r[h, g, ab, :, 0:gw], m2r[h, g, ab, :, gw:]
            )

    vocab_start = col * width
    lane = lax.broadcasted_iota(I32, (16, 128), 1)
    cb = min(1024, width)

    def softmax_part(h):
        for ab in range(2):
            rows = slice(ab * 16, ab * 16 + 16)
            q = own[ab] // 16
            inv_col = inv[q, h * 16:h * 16 + 16, 0:1]
            t_col = tgt[h, pl.ds(al(own[ab]), 16), 0:1] - vocab_start
            top = jnp.full((16, 1), -jnp.inf, F32)
            for n in range(width // cb):
                cols = slice(n * cb, (n + 1) * cb)
                x = logit[h, rows, cols] * inv_col
                top = jnp.maximum(top, jnp.max(x, axis=1, keepdims=True))
            total = jnp.zeros((16, 1), F32)
            moment = jnp.zeros((16, 1), F32)
            target = jnp.zeros((16, 1), F32)
            for n in range(width // cb):
                cols = slice(n * cb, (n + 1) * cb)
                x = logit[h, rows, cols] * inv_col
                y = jnp.exp(x - top)
                e[h, pl.ds(al(own[ab]), 16), cols] = y.astype(BF)
                total += jnp.sum(y, axis=1, keepdims=True)
                moment += jnp.sum(y * x, axis=1, keepdims=True)
                ids = lax.broadcasted_iota(I32, (16, cb), 1) + n * cb
                target += jnp.sum(jnp.where(ids == t_col, x, 0.0), axis=1, keepdims=True)
            send(c_e1, h, ab)
            st[h, col, rows, :] = jnp.where(
                lane == 0, top, jnp.where(lane == 1, total, jnp.where(lane == 2, moment, target))
            )
        send(c_st, h, peers=COLS)

    def spread_first(h):
        for ab in range(2):
            arrive(c_e1, h, ab)
            send(c_e2, h, ab)
        for ab in range(2):
            send(c_e3, h, ab, 0)

    def spread_second(h):
        for ab in range(2):
            arrive(c_e2, h, ab)
            send(c_e3, h, ab, 1)

    def combine(h):
        arrive(c_st, h, peers=COLS)
        top = st[h, 0, :, 0:1]
        for j in range(1, COLS):
            top = jnp.maximum(top, st[h, j, :, 0:1])
        total, moment, target = (jnp.zeros((32, 1), F32) for _ in range(3))
        for j in range(COLS):
            s = st[h, j]
            scale = jnp.exp(s[:, 0:1] - top)
            total += s[:, 1:2] * scale
            moment += s[:, 2:3] * scale
            target += s[:, 3:4]
        mine = jnp.exp(st[h, col, :, 0:1] - top) / total
        curv = moment / total - target
        for ab in range(2):
            rows = slice(ab * 16, ab * 16 + 16)
            inv_col = inv[own[ab] // 16, h * 16:h * 16 + 16, 0:1]
            fac[h, row, rows, :] = jnp.where(lane == 0, mine[rows] * inv_col, curv[rows])
        send(c_fa, h, peers=ROWS)

    def prepare(h, whose):
        for ab in range(2):
            for late in range(2):
                if whose:
                    arrive(c_e3, h, ab, late)
        if not whose:
            arrive(c_fa, h, peers=ROWS)

        def group(t, carry):
            q = (k + whose - 2 * k * whose) * 8 + t
            r, ab = owner_row(q)
            f_col = fac[h, r, pl.ds(al(ab * 16), 16), 0:1]
            inv_col = inv[q, h * 16:h * 16 + 16, 0:1]
            rows = pl.ds(al(q * 16), 16)
            t_col = tgt[h, rows, 0:1] - vocab_start
            for n in range(width // cb):
                cols = slice(n * cb, (n + 1) * cb)
                ids = lax.broadcasted_iota(I32, (16, cb), 1) + n * cb
                v = e[h, rows, cols].astype(F32) * f_col - jnp.where(ids == t_col, inv_col, 0.0)
                grad[h, rows, cols] = v.astype(BF)
            return carry

        lax.fori_loop(0, 8, group, 0)

    def product(h):
        for n in range(2):
            half = grad.at[h, :, n * width // 2:(n + 1) * width // 2]
            store(half, (grad_a, grad_b, grad_c, grad_d)[2 * h + n], out_sem.at[4 + 2 * h + n])

        for n in range(feats // 256):
            rows = slice(n * 256, (n + 1) * 256)
            v = lax.dot_general(grad[h], w[rows, :], NT, preferred_element_type=F32)
            fg[h, :, :, :, rows] = v.astype(BF).reshape(SIDE, SIDE, SUB, 256)
            if n == feats // 512 - 1:
                send(c_ra, h, peers=SIDE)
        send(c_rb, h, peers=SIDE)

    def sum_first(h):
        arrive(c_ra, h, peers=SIDE)
        total = fg[h, :, x, :, 0:hf].astype(F32)
        for i in range(1, SIDE):
            total = total + ra[h, i].astype(F32)
        ra[h, 0] = total.astype(BF)
        send(c_rc, h, peers=SIDE)
        arrive(c_rb, h, peers=SIDE)
        total = fg[h, y, :, :, hf:feats].astype(F32)
        for i in range(1, SIDE):
            total = total + rb[h, i].astype(F32)
        rb[h, 0] = total.astype(BF)
        send(c_rd, h, peers=SIDE)

    def residual(h):
        r, ab = owner_row(col)
        curv = fac[h, r, pl.ds(al(ab * 16), 16), 1:2]
        inv_col = inv[col, h * 16:h * 16 + 16, 0:1]
        factor = inv_col * inv_col * curv
        for half in range(2):
            cols = slice(half * hf, (half + 1) * hf)
            arrive((c_rc, c_rd)[half], h, peers=SIDE)
            total = (rb[h, 0, x] if half else ra[h, 0, y]).astype(F32)
            for i in range(1, SIDE):
                total = total + (rc, rd)[half][h, i].astype(F32)
            wide = hid[h * 16:h * 16 + 16, cols].astype(F32)
            v = (gain[:, cols] * total - wide * factor / D).astype(BF)
            gh[y, x, h, :, cols] = v
            own_out[h * 16:h * 16 + 16, cols] = v
            send((c_ga, c_gb)[half], h, peers=SIDE)

    def pass_on(h):
        arrive(c_ga, h, peers=SIDE)
        send(c_gc, h, peers=SIDE)
        arrive(c_gb, h, peers=SIDE)
        send(c_gd, h, peers=SIDE)

    def enter():
        for n in range(3, 6):
            store(*loads[n])
        for n in range(3):
            store(*loads[n])
        barrier = pltpu.get_barrier_semaphore()
        each(COLS, lambda i: pl.semaphore_signal(barrier, inc=1, device_id=col_dev(i), device_id_type=MESH))
        each(ROWS, lambda i: pl.semaphore_signal(barrier, inc=1, device_id=row_dev(i), device_id_type=MESH))
        for n in range(3, 6):
            stored(n)
        for h in range(2):
            v = hid[h * 16:h * 16 + 16, :].astype(F32)
            ag[h, y, x] = (gain[...] * v).astype(BF)
            sq[row, h * 16:h * 16 + 16, :] = jnp.broadcast_to(jnp.sum(v * v, axis=1, keepdims=True), (16, 128))
        pl.semaphore_wait(barrier, COLS + ROWS - 2)
        send(c_aa, 0, peers=SIDE)
        send(c_ab, 0, peers=SIDE)
        send(c_sq, peers=ROWS)

    def order_targets():
        ids = jnp.concatenate([tgt_in[...], tgt_in[...]], axis=0).astype(F32).T
        for j in range(COLS):
            for h in range(2):
                at = (j % 4) * 32 + h * 16
                ids_col = ids[at:at + 16, j // 4:j // 4 + 1].astype(I32)
                tgt[h, j * 16:j * 16 + 16, :] = jnp.broadcast_to(ids_col, (16, 128))

    def squares():
        arrive(c_sq, peers=ROWS)
        total = sq[0]
        for r in range(1, ROWS):
            total = total + sq[r]
        inv[col] = 1.0 / jnp.sqrt(total / D + EPS)
        send(c_inv, peers=COLS)

    def activate():
        stored(1)
        stored(2)

        @pl.loop(0, gate.shape[1] // 128)
        def _(n):
            cols = pl.ds(al(n * 128, 128), 128)
            v = gate[:, cols].astype(F32)
            act[cols, :] = (v / (1.0 + jnp.exp(-v)) * up[:, cols].astype(F32)).T.astype(BF)

        store(act, act_out, out_sem.at[1])

    def turn(h):
        at = slice(h * HALF, (h + 1) * HALF)
        for n in range(feats // 256):
            rows = slice(n * 256, (n + 1) * 256)
            turned[rows, at] = ag[h, :, :, :, rows].reshape(HALF, 256).T
        if h == 1:
            store(turned, scaled_out, out_sem.at[2])

    def gather_on(h):
        arrive(c_aa, h, peers=SIDE)
        send(c_ac, h, peers=SIDE)
        arrive(c_ab, h, peers=SIDE)
        send(c_ad, h, peers=SIDE)
        if h == 0:
            send(c_aa, 1, peers=SIDE)
            send(c_ab, 1, peers=SIDE)

    def gathered(h):
        arrive(c_ac, h, peers=SIDE)
        arrive(c_ad, h, peers=SIDE)

    def scales():
        arrive(c_inv, peers=COLS)

    def finish():
        for h in range(2):
            arrive(c_gc, h, peers=SIDE)
            arrive(c_gd, h, peers=SIDE)
        store(gh, all_out, out_sem.at[3])

    steps = [
        (enter,), (gather_on, 0), (order_targets,), (activate,), (stored, 0),
        (gathered, 0), (logits_part, 0, 0), (gather_on, 1), (logits_part, 0, 1), (reduce_core, 0, 0),
        (reduce_core, 0, 1), (squares,), (gathered, 1), (logits_part, 1, 0), (reduce_first, 0, 0), (logits_part, 1, 1),
        (reduce_first, 0, 1), (reduce_core, 1, 0), (reduce_core, 1, 1), (turn, 0), (turn, 1),
        (scales,), (reduce_second, 0, 0), (reduce_second, 0, 1), (softmax_part, 0),
        (reduce_first, 1, 0), (reduce_first, 1, 1), (spread_first, 0),
        (reduce_second, 1, 0), (reduce_second, 1, 1), (softmax_part, 1),
        (combine, 0), (spread_second, 0), (spread_first, 1), (prepare, 0, 0), (prepare, 0, 1), (combine, 1),
        (product, 0), (spread_second, 1), (prepare, 1, 0), (prepare, 1, 1), (product, 1),
        (sum_first, 0), (residual, 0), (sum_first, 1), (pass_on, 0), (residual, 1), (pass_on, 1), (finish,),
    ]
    for step, *which in steps[:STOP]:
        step(*which)
    for make, key, peers in list(coming):
        arrive(make, *key, peers=peers)
    for make, key, peers in started:
        left(make, key, peers)
    for src, dst, sem in stores:
        pltpu.make_async_copy(src, dst, sem).wait()


def weights_kernel(scaled, grad_a, grad_b, grad_c, grad_d, act, resid, head, down):
    i = pl.program_id(0)
    width = head.shape[1]
    at = pl.ds(pl.multiple_of((i % (pl.num_programs(0) // 2)) * width, 128), width)

    def tile(first, second):
        total = jnp.dot(scaled[:, :HALF], first[:, at], preferred_element_type=F32)
        head[...] = (total + jnp.dot(scaled[:, HALF:], second[:, at], preferred_element_type=F32)).astype(BF)

    @pl.when(i < pl.num_programs(0) // 2)
    def _():
        tile(grad_a, grad_c)

    @pl.when(i >= pl.num_programs(0) // 2)
    def _():
        tile(grad_b, grad_d)

    down[...] = jnp.dot(act[...], resid[...], preferred_element_type=F32).astype(BF)


def on_device(hidden_state, norm_gain, head_weight, targets, gate_act, up_act):
    feats, width = head_weight.shape
    gw = width // G
    tokens = 2 * HALF
    hidden_units = gate_act.shape[1]
    vm, hbm = pl.BlockSpec(memory_space=pltpu.VMEM), pl.BlockSpec(memory_space=pl.ANY)
    dma = pltpu.SemaphoreType.DMA

    def pair(*shape):
        return [dma(shape), dma(shape)]

    grad_hidden, *grads, scaled, resid, act = pl.pallas_call(
        kernel,
        out_shape=(
            jax.ShapeDtypeStruct(hidden_state.shape, BF),
            *[jax.ShapeDtypeStruct((HALF, width // 2), BF)] * 4,
            jax.ShapeDtypeStruct((feats, tokens), BF),
            jax.ShapeDtypeStruct((SIDE, SIDE, 2, SUB, feats), BF),
            jax.ShapeDtypeStruct((hidden_units, tokens), BF),
        ),
        in_specs=[pl.BlockSpec(memory_space=pltpu.HBM)] * 6,
        out_specs=(vm, *[hbm] * 7),
        scratch_shapes=[
            pltpu.VMEM(hidden_state.shape, BF),
            pltpu.VMEM((1, feats), F32),
            pltpu.VMEM((4, 128), I32),
            pltpu.VMEM((feats, width), BF),
            pltpu.VMEM((tokens, hidden_units), BF),
            pltpu.VMEM((tokens, hidden_units), BF),
            pltpu.VMEM((hidden_units, tokens), BF),
            pltpu.VMEM((feats, tokens), BF),
            pltpu.VMEM((2, HALF, 128), I32),
            pltpu.VMEM((2, SIDE, SIDE, SUB, feats), BF),
            pltpu.VMEM((ROWS, 32, 128), F32),
            pltpu.VMEM((COLS, 32, 128), F32),
            pltpu.VMEM((2, G, HALF, gw), F32),
            pltpu.VMEM((2, G, HALF // 2, gw), F32),
            pltpu.VMEM((2, G, 2, 32, gw + TAIL), I16),
            pltpu.VMEM((2, G, 2, 32, gw + TAIL), I16),
            pltpu.VMEM((2, G, 2, 16, gw + TAIL), I16),
            pltpu.VMEM((2, G, 2, 16, gw + TAIL), I16),
            pltpu.VMEM((2, 32, width), F32),
            pltpu.VMEM((2, HALF, width), BF),
            pltpu.VMEM((2, HALF, width), BF),
            pltpu.VMEM((2, COLS, 32, 128), F32),
            pltpu.VMEM((2, ROWS, 32, 128), F32),
            pltpu.VMEM((2, SIDE, SIDE, SUB, feats), BF),
            pltpu.VMEM((2, SIDE, SIDE, SUB, feats // 2), BF),
            pltpu.VMEM((2, SIDE, SIDE, SUB, feats // 2), BF),
            pltpu.VMEM((2, SIDE, SUB, feats // 2), BF),
            pltpu.VMEM((2, SIDE, SUB, feats // 2), BF),
            pltpu.VMEM((SIDE, SIDE, 2, SUB, feats), BF),
            dma((6,)), dma((8,)),
            *pair(ROWS), *pair(COLS), *pair(2, G, gw // PIECE), *pair(2, G, 2), *pair(2, G, 2),
            *pair(2, 2), *pair(2, 2), *pair(2, 2, 2), *pair(2, COLS), *pair(2, ROWS),
            *[dma((2, SIDE))] * 24,
        ],
        compiler_params=pltpu.CompilerParams(
            collective_id=0, has_side_effects=True, vmem_limit_bytes=46 * 2**20
        ),
        name="head_backward",
    )(hidden_state, norm_gain.reshape(1, feats), targets.reshape(4, 128), head_weight, gate_act, up_act)
    tiles = 8
    head_grad, down_grad = pl.pallas_call(
        weights_kernel,
        grid=(tiles,),
        out_shape=(
            jax.ShapeDtypeStruct((feats, width), BF),
            jax.ShapeDtypeStruct((hidden_units, feats), BF),
        ),
        in_specs=[vm] * 5 + [pl.BlockSpec((hidden_units // tiles, tokens), lambda i: (i, 0)), vm],
        out_specs=(
            pl.BlockSpec((feats, width // tiles), lambda i: (0, i)),
            pl.BlockSpec((hidden_units // tiles, feats), lambda i: (i, 0)),
        ),
        compiler_params=pltpu.CompilerParams(vmem_limit_bytes=24 * 2**20),
        name="weight_gradients",
    )(scaled, *grads, act, resid.reshape(tokens, feats))
    return head_grad, grad_hidden, down_grad


def solution(mesh):
    in_specs = (P("col", "row"), P("row"), P("row", "col"), P(), P(None, "col"), P(None, "col"))
    out_specs = (P("row", "col"), P("col", "row"), P("col", "row"))
    return jax.shard_map(
        on_device, mesh=mesh, in_specs=in_specs, out_specs=out_specs, check_vma=False
    )
```

time: 118 us -> 105 us (0.89)
  matrix products: 14.6 us -> 0 us
    dot_general x2 -> x0, matrix products: 14.6 us -> none  [the longest x1 10.6 us: on_device(): lax.dot_general(scaled.reshape(tokens, feats), grad.reshape(tokens, width...]
    pallas_call x0 -> x1, Pallas kernels: none -> 9.98 us  [on_device(): pl.pallas_call(weights_kernel, grid=(tiles,), out_shape=(jax.ShapeDtypeSt...]
    pallas_call x1, Pallas kernels: 100 us -> 91.4 us  [on_device(): pl.pallas_call(kernel, out_shape=(jax.ShapeDtypeStruct(hidden_state.shape...]
    unnamed x9 -> x7, local copies, waits for them, and re-layouts: 0.65 us -> 2.83 us
where the time goes in v2:
time: 105 us
  Pallas kernels  101 us (96%)
  local copies, waits for them, and re-layouts  2.83 us (3%)
    pallas_call x1, Pallas kernels, on_device(): pl.pallas_call(kernel, out_shape=(jax.ShapeDtypeStruct(hidden_state.shape...  91.4 us
    pallas_call x1, Pallas kernels, on_device(): pl.pallas_call(weights_kernel, grid=(tiles,), out_shape=(jax.ShapeDtypeSt...  9.98 us
    unnamed x7, local copies, waits for them, and re-layouts  2.83 us

profile of v2, /device:TPU:0, one launch (start us, length us, event | category | flops | bytes accessed | tf_op | source)
XLA Modules:
  0.0 104.8 jit_solution(9546054670466672871)
XLA Ops:
  0.6 0.0 copy-start
  0.6 0.8 copy-done
  1.5 0.0 copy-start.1
  1.5 0.7 copy-done.1
  2.2 0.0 copy-start.2
  2.2 0.7 copy-done.2
  2.8 91.4 %head_backward.1 = (bf16[32,1024]{1,0:T(8,128)(2,1)S(1)}, bf16[256,2048]{1,0:T(8,128)(2,1)S(1)}, bf16[256,2048]{1,0:T(8,128)(2,1)S(1)}, bf16[256,2048]{1,0:T(8,1...) custom-call(bf16[32,1024]{1,0:T(8,128)(2,1)S(1)} %copy-done, ...), custom_call_target="tpu_custom_call" | custom-call | tf_op jit(solution)/shard_map/head_backward/pallas_call | solution.py:526
  94.2 10.0 %weight_gradients.1 = (bf16[1024,4096]{1,0:T(8,128)(2,1)}, bf16[1664,1024]{1,0:T(8,128)(2,1)}) custom-call(bf16[1024,512]{1,0:T(8,128)(2,1)S(1)} %get-tuple-element.13.scaled, bf16[256,2048]{1,0:T(8,128)(2,1)S(1)} %get-tuple-element.14.grad_a, bf16[256,2048]{1,0:T(8,128)(2,1)S(1)} %get-tuple-element.15.grad_b, ...), custom_call_target="tpu_custom_call" | custom-call | tf_op jit(solution)/shard_map/weight_gradients/pallas_call | solution.py:578
  104.2 0.6 copy.10
Async XLA Ops:
  0.6 0.8 copy-start
  1.5 0.7 copy-start.1
  2.2 0.7 copy-start.2

commit v3 on v2

--- a/solution.py
+++ b/solution.py
@@ -12,6 +12,7 @@
 COLS, ROWS = 16, 8
 SIDE = 4
 PIECE = 512
+QUARTERS = 4
 G = 2
 SUB = 16
 HALF = SUB * COLS
@@ -43,7 +44,7 @@
 
 def kernel(
     hid_hbm, gain_hbm, tgt_hbm, w_hbm, gate_hbm, up_hbm,
-    own_out, grad_a, grad_b, grad_c, grad_d, scaled_out, all_out, act_out,
+    grad_a, grad_b, grad_c, grad_d, scaled_out, all_out, act_out,
     hid, gain, tgt_in, w, gate, up, act, turned, tgt, ag, sq, inv, part, core, m1s, m1r, m2s, m2r, logit, e, grad, st, fac, fg, ra, rb, rc, rd, gh,
     in_sem, out_sem, sq_s, sq_r, inv_s, inv_r, c_s, c_r, z1_s, z1_r, z2_s, z2_r,
     e1_s, e1_r, e2_s, e2_r, e3_s, e3_r, st_s, st_r, fa_s, fa_r,
@@ -344,9 +345,9 @@
         lax.fori_loop(0, 8, group, 0)
 
     def product(h):
-        for n in range(2):
-            half = grad.at[h, :, n * width // 2:(n + 1) * width // 2]
-            store(half, (grad_a, grad_b, grad_c, grad_d)[2 * h + n], out_sem.at[4 + 2 * h + n])
+        for n in range(QUARTERS):
+            block = grad.at[h, :, n * width // QUARTERS:(n + 1) * width // QUARTERS]
+            store(block, (grad_a, grad_b, grad_c, grad_d)[n].at[h], out_sem.at[3 + QUARTERS * h + n])
 
         for n in range(feats // 256):
             rows = slice(n * 256, (n + 1) * 256)
@@ -384,7 +385,6 @@
             wide = hid[h * 16:h * 16 + 16, cols].astype(F32)
             v = (gain[:, cols] * total - wide * factor / D).astype(BF)
             gh[y, x, h, :, cols] = v
-            own_out[h * 16:h * 16 + 16, cols] = v
             send((c_ga, c_gb)[half], h, peers=SIDE)
 
     def pass_on(h):
@@ -468,7 +468,7 @@
         for h in range(2):
             arrive(c_gc, h, peers=SIDE)
             arrive(c_gd, h, peers=SIDE)
-        store(gh, all_out, out_sem.at[3])
+        store(gh, all_out, out_sem.at[0])
 
     steps = [
         (enter,), (gather_on, 0), (order_targets,), (activate,), (stored, 0),
@@ -492,24 +492,20 @@
         pltpu.make_async_copy(src, dst, sem).wait()
 
 
-def weights_kernel(scaled, grad_a, grad_b, grad_c, grad_d, act, resid, head, down):
+def weights_kernel(scaled, grad_a, grad_b, grad_c, grad_d, act, resid, head, down, own):
     i = pl.program_id(0)
-    width = head.shape[1]
-    at = pl.ds(pl.multiple_of((i % (pl.num_programs(0) // 2)) * width, 128), width)
-
-    def tile(first, second):
-        total = jnp.dot(scaled[:, :HALF], first[:, at], preferred_element_type=F32)
-        head[...] = (total + jnp.dot(scaled[:, HALF:], second[:, at], preferred_element_type=F32)).astype(BF)
-
-    @pl.when(i < pl.num_programs(0) // 2)
+    for n, grad in enumerate((grad_a, grad_b, grad_c, grad_d)):
+
+        @pl.when(i == n)
+        def _(grad=grad):
+            block = grad[...].reshape(2 * HALF, head.shape[1])
+            head[...] = jnp.dot(scaled[...], block, preferred_element_type=F32).astype(BF)
+
+    down[...] = jnp.dot(act[...], resid[...], preferred_element_type=F32).astype(BF)
+
+    @pl.when(i == 0)
     def _():
-        tile(grad_a, grad_c)
-
-    @pl.when(i >= pl.num_programs(0) // 2)
-    def _():
-        tile(grad_b, grad_d)
-
-    down[...] = jnp.dot(act[...], resid[...], preferred_element_type=F32).astype(BF)
+        own[...] = resid[pl.ds(pl.multiple_of(lax.axis_index("col") * 32, 32), 32), :]
 
 
 def on_device(hidden_state, norm_gain, head_weight, targets, gate_act, up_act):
@@ -523,17 +519,16 @@
     def pair(*shape):
         return [dma(shape), dma(shape)]
 
-    grad_hidden, *grads, scaled, resid, act = pl.pallas_call(
+    *grads, scaled, resid, act = pl.pallas_call(
         kernel,
         out_shape=(
-            jax.ShapeDtypeStruct(hidden_state.shape, BF),
-            *[jax.ShapeDtypeStruct((HALF, width // 2), BF)] * 4,
+            *[jax.ShapeDtypeStruct((2, HALF, width // QUARTERS), BF)] * QUARTERS,
             jax.ShapeDtypeStruct((feats, tokens), BF),
             jax.ShapeDtypeStruct((SIDE, SIDE, 2, SUB, feats), BF),
             jax.ShapeDtypeStruct((hidden_units, tokens), BF),
         ),
         in_specs=[pl.BlockSpec(memory_space=pltpu.HBM)] * 6,
-        out_specs=(vm, *[hbm] * 7),
+        out_specs=(*[hbm] * 7,),
         scratch_shapes=[
             pltpu.VMEM(hidden_state.shape, BF),
             pltpu.VMEM((1, feats), F32),
@@ -564,7 +559,7 @@
             pltpu.VMEM((2, SIDE, SUB, feats // 2), BF),
             pltpu.VMEM((2, SIDE, SUB, feats // 2), BF),
             pltpu.VMEM((SIDE, SIDE, 2, SUB, feats), BF),
-            dma((6,)), dma((8,)),
+            dma((6,)), dma((11,)),
             *pair(ROWS), *pair(COLS), *pair(2, G, gw // PIECE), *pair(2, G, 2), *pair(2, G, 2),
             *pair(2, 2), *pair(2, 2), *pair(2, 2, 2), *pair(2, COLS), *pair(2, ROWS),
             *[dma((2, SIDE))] * 24,
@@ -574,18 +569,20 @@
         ),
         name="head_backward",
     )(hidden_state, norm_gain.reshape(1, feats), targets.reshape(4, 128), head_weight, gate_act, up_act)
-    tiles = 8
-    head_grad, down_grad = pl.pallas_call(
+    tiles = QUARTERS
+    head_grad, down_grad, grad_hidden = pl.pallas_call(
         weights_kernel,
         grid=(tiles,),
         out_shape=(
             jax.ShapeDtypeStruct((feats, width), BF),
             jax.ShapeDtypeStruct((hidden_units, feats), BF),
+            jax.ShapeDtypeStruct(hidden_state.shape, BF),
         ),
         in_specs=[vm] * 5 + [pl.BlockSpec((hidden_units // tiles, tokens), lambda i: (i, 0)), vm],
         out_specs=(
             pl.BlockSpec((feats, width // tiles), lambda i: (0, i)),
             pl.BlockSpec((hidden_units // tiles, feats), lambda i: (i, 0)),
+            pl.BlockSpec(hidden_state.shape, lambda i: (0, 0)),
         ),
         compiler_params=pltpu.CompilerParams(vmem_limit_bytes=24 * 2**20),
         name="weight_gradients",

time: 105 us -> 104 us (level)
    unnamed x7 -> x6, local copies, waits for them, and re-layouts: 2.83 us -> 2.2 us
where the time goes in v3:
time: 104 us; the launch traced here: 103 us
  Pallas kernels  101 us (97%)
  local copies, waits for them, and re-layouts  2.2 us (2%)
    pallas_call x1, Pallas kernels, on_device(): pl.pallas_call(kernel, out_shape=(*[jax.ShapeDtypeStruct((2, HALF, width...  91.4 us
    pallas_call x1, Pallas kernels, on_device(): pl.pallas_call(weights_kernel, grid=(tiles,), out_shape=(jax.ShapeDtypeSt...  9.2 us
    unnamed x6, local copies, waits for them, and re-layouts  2.2 us

profile of v3, /device:TPU:0, one launch (start us, length us, event | category | flops | bytes accessed | tf_op | source)
XLA Modules:
  0.0 103.5 jit_solution(4845153755082368807)
XLA Ops:
  0.6 0.0 copy-start
  0.6 0.8 copy-done
  1.5 0.0 copy-start.1
  1.5 0.7 copy-done.1
  2.2 0.0 copy-start.2
  2.2 0.7 copy-done.2
  2.8 91.4 %head_backward.1 = (bf16[2,256,1024]{2,1,0:T(8,128)(2,1)S(1)}, bf16[2,256,1024]{2,1,0:T(8,128)(2,1)S(1)}, bf16[2,256,1024]{2,1,0:T(8,128)(2,1)S(1)}, bf16[2,256,...) custom-call(bf16[32,1024]{1,0:T(8,128)(2,1)S(1)} %copy-done, ...), custom_call_target="tpu_custom_call" | custom-call | tf_op jit(solution)/shard_map/head_backward/pallas_call | solution.py:522
  94.3 9.2 %weight_gradients.1 = (bf16[1024,4096]{1,0:T(8,128)(2,1)}, bf16[1664,1024]{1,0:T(8,128)(2,1)}, bf16[32,1024]{1,0:T(8,128)(2,1)}) custom-call(bf16[1024,512]{1,0:T(8,128)(2,1)S(1)} %get-tuple-element.13.scaled, bf16[2,256,1024]{2,1,0:T(8,128)(2,1)S(1)} %get-tuple-element.14.grad_a, bf16[2,256,1024]{2,1,0:T(8,128)(2,1)S(1)} %get-tuple-element.15.grad_b, ...), custom_call_target="tpu_custom_call" | custom-call | tf_op jit(solution)/shard_map/weight_gradients/pallas_call | solution.py:573
Async XLA Ops:
  0.6 0.8 copy-start
  1.5 0.7 copy-start.1
  2.2 0.7 copy-start.2

commit v4 on v3

--- a/solution.py
+++ b/solution.py
@@ -344,18 +344,16 @@
 
         lax.fori_loop(0, 8, group, 0)
 
-    def product(h):
-        for n in range(QUARTERS):
-            block = grad.at[h, :, n * width // QUARTERS:(n + 1) * width // QUARTERS]
-            store(block, (grad_a, grad_b, grad_c, grad_d)[n].at[h], out_sem.at[3 + QUARTERS * h + n])
-
-        for n in range(feats // 256):
+    def product(h, half):
+        if half == 0:
+            for n in range(QUARTERS):
+                block = grad.at[h, :, n * width // QUARTERS:(n + 1) * width // QUARTERS]
+                store(block, (grad_a, grad_b, grad_c, grad_d)[n].at[h], out_sem.at[3 + QUARTERS * h + n])
+        for n in range(half * hf // 256, (half + 1) * hf // 256):
             rows = slice(n * 256, (n + 1) * 256)
             v = lax.dot_general(grad[h], w[rows, :], NT, preferred_element_type=F32)
             fg[h, :, :, :, rows] = v.astype(BF).reshape(SIDE, SIDE, SUB, 256)
-            if n == feats // 512 - 1:
-                send(c_ra, h, peers=SIDE)
-        send(c_rb, h, peers=SIDE)
+        send((c_ra, c_rb)[half], h, peers=SIDE)
 
     def sum_first(h):
         arrive(c_ra, h, peers=SIDE)
@@ -479,7 +477,7 @@
         (reduce_first, 1, 0), (reduce_first, 1, 1), (spread_first, 0),
         (reduce_second, 1, 0), (reduce_second, 1, 1), (softmax_part, 1),
         (combine, 0), (spread_second, 0), (spread_first, 1), (prepare, 0, 0), (prepare, 0, 1), (combine, 1),
-        (product, 0), (spread_second, 1), (prepare, 1, 0), (prepare, 1, 1), (product, 1),
+        (product, 0, 0), (spread_second, 1), (product, 0, 1), (prepare, 1, 0), (prepare, 1, 1), (product, 1, 0), (product, 1, 1),
         (sum_first, 0), (residual, 0), (sum_first, 1), (pass_on, 0), (residual, 1), (pass_on, 1), (finish,),
     ]
     for step, *which in steps[:STOP]:

time: 104 us -> 103 us (level)
  no operation moved by 1% of the time
where the time goes in v4:
time: 103 us
  Pallas kernels  100 us (97%)
  local copies, waits for them, and re-layouts  2.2 us (2%)
    pallas_call x1, Pallas kernels, on_device(): pl.pallas_call(kernel, out_shape=(*[jax.ShapeDtypeStruct((2, HALF, width...  91.1 us
    pallas_call x1, Pallas kernels, on_device(): pl.pallas_call(weights_kernel, grid=(tiles,), out_shape=(jax.ShapeDtypeSt...  9.2 us
    unnamed x6, local copies, waits for them, and re-layouts  2.2 us

profile of v4, /device:TPU:0, one launch (start us, length us, event | category | flops | bytes accessed | tf_op | source)
XLA Modules:
  0.0 103.2 jit_solution(1064209372281730932)
XLA Ops:
  0.6 0.0 copy-start
  0.6 0.8 copy-done
  1.5 0.0 copy-start.1
  1.5 0.7 copy-done.1
  2.2 0.0 copy-start.2
  2.2 0.7 copy-done.2
  2.8 91.1 %head_backward.1 = (bf16[2,256,1024]{2,1,0:T(8,128)(2,1)S(1)}, bf16[2,256,1024]{2,1,0:T(8,128)(2,1)S(1)}, bf16[2,256,1024]{2,1,0:T(8,128)(2,1)S(1)}, bf16[2,256,...) custom-call(bf16[32,1024]{1,0:T(8,128)(2,1)S(1)} %copy-done, ...), custom_call_target="tpu_custom_call" | custom-call | tf_op jit(solution)/shard_map/head_backward/pallas_call | solution.py:520
  94.0 9.2 %weight_gradients.1 = (bf16[1024,4096]{1,0:T(8,128)(2,1)}, bf16[1664,1024]{1,0:T(8,128)(2,1)}, bf16[32,1024]{1,0:T(8,128)(2,1)}) custom-call(bf16[1024,512]{1,0:T(8,128)(2,1)S(1)} %get-tuple-element.13.scaled, bf16[2,256,1024]{2,1,0:T(8,128)(2,1)S(1)} %get-tuple-element.14.grad_a, bf16[2,256,1024]{2,1,0:T(8,128)(2,1)S(1)} %get-tuple-element.15.grad_b, ...), custom_call_target="tpu_custom_call" | custom-call | tf_op jit(solution)/shard_map/weight_gradients/pallas_call | solution.py:571
Async XLA Ops:
  0.6 0.8 copy-start
  1.5 0.7 copy-start.1
  2.2 0.7 copy-start.2
